TPU v7x, 256 devices: a whole 4x4x8 slice. The times are simulated.
256 devices in a mesh: sect: 2 (over z_lo), dp: 32 (over z_hi, x, core), tp: 4 (over y).
Axes of the slice: x: 4, y: 4, z: 8 (z_hi: 4, z_lo: 2; z = z_hi * 2 + z_lo), core: 2. Of those that a mesh axis runs over, the one named last changes fastest.
Arguments:
- w_key: bfloat16 [8192, 1024], P(('sect', 'dp', 'tp')), may hold values from -0.0625 to 0.0625
- w_value: bfloat16 [8192, 1024], P(('sect', 'dp', 'tp')), may hold values from -0.0625 to 0.0625
- hidden: bfloat16 [256, 16, 8192], P(('sect', 'dp'), None, 'tp'), may hold values from -6 to 6
- queries: bfloat16 [256, 16, 8192], P(('sect', 'dp'), None, 'tp'), may hold values from -36 to 36
- key_cache: bfloat16 [256, 512, 1024], P(('sect', 'dp'), None, 'tp'), may hold values from -6 to 6
- value_cache: bfloat16 [256, 512, 1024], P(('sect', 'dp'), None, 'tp'), may hold values from -6 to 6
- prompt_lengths: int32 [256], P(('sect', 'dp')), may hold values from 64 to 512
- rollout_lengths: int32 [256], P(('sect', 'dp')), may hold values from 1 to 16
- batch_slots: int32 [256], replicated, may hold values from 0 to 255, as said below
Outputs:
- batched: bfloat16 [256, 16, 8192], P(('sect', 'dp'), None, 'tp')
Inputs may be any that keep to these rules, and one draw needn't show every extreme that they name: `batch_slots`: every row number appears once; a holder owns 4 consecutive rows of the micro-batch order, and the 4 sequences of one index of sect and dp go to 4 different holders.
All inputs are finite; a program needn't handle non-finite values.
Results may differ from a plain program's by a relative error of at most 0.0059.
Values may be sent and summed in bfloat16 or wider, within the bound.
A program may use at most 64 MiB of HBM per device.

v0:
```python
import jax
import jax.numpy as jnp
from jax import lax
from jax.sharding import PartitionSpec as P

D = 8192
HEAD = 128
STEPS = 16
CTX = 512
GROUP = 8


def attend(queries, new_keys, new_values, key_cache, value_cache, prompt_lengths, rollout_lengths):
    count = queries.shape[0]
    heads_kv = key_cache.shape[2] // HEAD
    scale = HEAD ** (-0.5)
    query = queries.reshape(count, STEPS, heads_kv, GROUP, HEAD)
    cache_k = key_cache.reshape(count, CTX, heads_kv, HEAD)
    cache_v = value_cache.reshape(count, CTX, heads_kv, HEAD)
    fresh_k = new_keys.reshape(count, STEPS, heads_kv, HEAD)
    fresh_v = new_values.reshape(count, STEPS, heads_kv, HEAD)
    live = (jnp.arange(CTX)[None, :] < prompt_lengths[:, None])[:, None, None, None, :]
    causal = (jnp.arange(STEPS)[None, :] <= jnp.arange(STEPS)[:, None])[None, :, None, None, :]
    score_c = (
        jnp.einsum("nikgd,njkd->nikgj", query, cache_k, preferred_element_type=jnp.float32) * scale
    )
    score_n = (
        jnp.einsum("nikgd,njkd->nikgj", query, fresh_k, preferred_element_type=jnp.float32) * scale
    )
    score_c = jnp.where(live, score_c, -1e30)
    score_n = jnp.where(causal, score_n, -1e30)
    top = jnp.maximum(jnp.max(score_c, axis=-1), jnp.max(score_n, axis=-1))
    exp_c = jnp.exp(score_c - top[..., None])
    exp_n = jnp.exp(score_n - top[..., None])
    total = jnp.sum(exp_c, axis=-1) + jnp.sum(exp_n, axis=-1)
    weight_c = (exp_c / total[..., None]).astype(jnp.bfloat16)
    weight_n = (exp_n / total[..., None]).astype(jnp.bfloat16)
    result = jnp.einsum("nikgj,njkd->nikgd", weight_c, cache_v, preferred_element_type=jnp.float32)
    result = result + jnp.einsum(
        "nikgj,njkd->nikgd", weight_n, fresh_v, preferred_element_type=jnp.float32
    )
    keep = (jnp.arange(STEPS)[None, :] < rollout_lengths[:, None])[:, :, None, None, None]
    result = jnp.where(keep, result, 0.0)
    return result.astype(jnp.bfloat16).reshape(count, STEPS, heads_kv * GROUP * HEAD)


def shards(
    w_key,
    w_value,
    hidden,
    queries,
    key_cache,
    value_cache,
    prompt_lengths,
    rollout_lengths,
    batch_slots,
):
    count = hidden.shape[0]
    whole = lax.all_gather(hidden, "tp", axis=2, tiled=True)
    flat = whole.reshape(count * STEPS, D)
    rows_key, rows_value = (
        lax.all_gather(w_key, ("sect", "dp"), axis=0, tiled=True),
        lax.all_gather(w_value, ("sect", "dp"), axis=0, tiled=True),
    )
    cols_key, cols_value = (
        lax.all_to_all(rows_key, "tp", split_axis=1, concat_axis=0, tiled=True),
        lax.all_to_all(rows_value, "tp", split_axis=1, concat_axis=0, tiled=True),
    )
    heads_tp = lax.axis_size("tp")
    groups = lax.axis_size(("sect", "dp"))
    block = w_key.shape[0]
    width = cols_key.shape[1]

    def reorder(a):
        return a.reshape(heads_tp, groups, block, width).transpose(1, 0, 2, 3).reshape(D, width)

    key_sum = jnp.dot(flat, reorder(cols_key), preferred_element_type=jnp.float32)
    value_sum = jnp.dot(flat, reorder(cols_value), preferred_element_type=jnp.float32)
    new_keys = key_sum.astype(jnp.bfloat16).reshape(count, STEPS, -1)
    new_values = value_sum.astype(jnp.bfloat16).reshape(count, STEPS, -1)
    attended = attend(
        queries, new_keys, new_values, key_cache, value_cache, prompt_lengths, rollout_lengths
    )
    owner = lax.axis_index(("sect", "dp"))
    targets = owner * count + jnp.arange(count, dtype=jnp.int32)
    select = (batch_slots[None, :] == targets[:, None]).astype(jnp.bfloat16)
    gathered = jnp.einsum(
        "rs,sid->rid",
        select,
        lax.all_gather(attended, ("sect", "dp"), axis=0, tiled=True),
        preferred_element_type=jnp.float32,
    )
    return gathered.astype(jnp.bfloat16)


def solution(mesh):
    in_specs = (
        P(("sect", "dp", "tp"), None),
        P(("sect", "dp", "tp"), None),
        P(("sect", "dp"), None, "tp"),
        P(("sect", "dp"), None, "tp"),
        P(("sect", "dp"), None, "tp"),
        P(("sect", "dp"), None, "tp"),
        P(("sect", "dp")),
        P(("sect", "dp")),
        P(),
    )
    out_specs = P(("sect", "dp"), None, "tp")
    return jax.shard_map(shards, mesh=mesh, in_specs=in_specs, out_specs=out_specs, check_vma=False)
```

profile of v0, /device:TPU:1, one launch (start us, length us, event | category | flops | bytes accessed | tf_op | source)
XLA Modules:
  0.0 486.6 jit_solution(5059575155432718921)
XLA Ops:
  6.5 0.7 all-gather.7.cloned.1.call-update
  7.3 0.7 all-gather.9.cloned.1.call-update
  8.0 121.7 %all-gather.7.cloned.1.call-done = bf16[2048,1024]{1,0:T(8,128)(2,1)} async-done(((bf16[32,1024]{1,0:T(8,128)(2,1)}), bf16[2048,1024]{1,0:T(8,128)(2,1)}) %all-gather.7.cloned.1.call-update) | async-done | bytes 4194320 | tf_op jit(solution)/shard_map/all_gather | solution.py:62
  129.7 6.5 %copy.64 = bf16[2048,1024]{0,1:T(8,128)(2,1)} copy(bf16[2048,1024]{1,0:T(8,128)(2,1)} %all-gather.7.cloned.1.call-done) | data formatting | bytes 8388608 | tf_op jit(solution)/shard_map/all_gather | solution.py:62
  136.2 4.9 %all-to-all-start = ((bf16[2048,4,256]{0,2,1:T(8,128)(2,1)}), bf16[2048,4,256]{0,2,1:T(8,128)(2,1)}, u32[]{:S(2)}, u32[]{:S(2)}) async-start(bf16[2048,4,256]{0,2,1:T(8,128)(2,1)} %bitcast.57), calls=%async_computation | async-start | bytes 8388608 | tf_op jit(solution)/shard_map/all_to_all | solution.py:66
  141.2 0.7 all-gather.5.cloned.1.call-update
  141.9 103.8 %all-gather.9.cloned.1.call-done = bf16[2048,1024]{1,0:T(8,128)(2,1)} async-done(((bf16[32,1024]{1,0:T(8,128)(2,1)}), bf16[2048,1024]{1,0:T(8,128)(2,1)}) %all-gather.9.cloned.1.call-update) | async-done | bytes 4194320 | tf_op jit(solution)/shard_map/all_gather | solution.py:63
  245.6 6.5 %copy.71 = bf16[2048,1024]{0,1:T(8,128)(2,1)} copy(bf16[2048,1024]{1,0:T(8,128)(2,1)} %all-gather.9.cloned.1.call-done) | data formatting | bytes 8388608 | tf_op jit(solution)/shard_map/all_gather | solution.py:63
  252.2 5.0 %all-to-all-start.1 = ((bf16[2048,4,256]{0,2,1:T(8,128)(2,1)}), bf16[2048,4,256]{0,2,1:T(8,128)(2,1)}, u32[]{:S(2)}, u32[]{:S(2)}) async-start(bf16[2048,4,256]{0,2,1:T(8,128)(2,1)} %bitcast.56), calls=%async_computation.1 | async-start | bytes 8388608 | tf_op jit(solution)/shard_map/all_to_all | solution.py:67
  257.3 1.2 reshape.100
  258.6 0.3 reshape.105
  259.0 1.8 bitcast_reduce_fusion
  260.8 6.2 %copy.65 = bf16[4,2048,256]{2,1,0:T(8,128)(2,1)} copy(bf16[4,2048,256]{1,2,0:T(8,128)(2,1)} %bitcast.5) | data formatting | bytes 8388608 | tf_op jit(solution)/shard_map/all_to_all | solution.py:66
  267.1 4.8 copy.66
  271.9 7.1 %all-gather.5.cloned.1.call-done = bf16[4,16,8192]{2,1,0:T(8,128)(2,1)} async-done(((bf16[4,16,2048]{2,1,0:T(8,128)(2,1)}), bf16[4,16,8192]{2,1,0:T(8,128)(2,1)}) %all-gather.5.cloned.1.call-update) | async-done | bytes 1048592 | tf_op jit(solution)/shard_map/all_gather | solution.py:59
  278.9 3.3 convolution_convert_fusion.1
  282.3 0.7 fusion.25
  283.2 0.6 fusion.6
  283.9 0.8 divide_convert_fusion.1
  284.7 1.2 copy.75
  285.9 1.6 divide_convert_fusion
  287.5 27.1 %all-to-all-done.1 = bf16[2048,4,256]{0,2,1:T(8,128)(2,1)} async-done(((bf16[2048,4,256]{0,2,1:T(8,128)(2,1)}), bf16[2048,4,256]{0,2,1:T(8,128)(2,1)}, u32[]{:S(2)}, u32[]{:S(2)}) %all-to-all-start.1) | async-done | bytes 4194336 | tf_op jit(solution)/shard_map/all_to_all | solution.py:67
  314.6 6.2 %copy.72 = bf16[4,2048,256]{2,1,0:T(8,128)(2,1)} copy(bf16[4,2048,256]{1,2,0:T(8,128)(2,1)} %bitcast.14) | data formatting | bytes 8388608 | tf_op jit(solution)/shard_map/all_to_all | solution.py:67
  320.8 2.7 copy.73
  323.6 0.8 convolution_convert_fusion
  324.4 0.2 convolution_bitcast_fusion.1
  324.6 0.2 copy-done.3
  324.8 0.8 fusion.11
  325.6 0.8 reshape.108
  326.5 129.3 %all-gather.11.cloned.1.call-done = bf16[256,16,2048]{2,1,0:T(8,128)(2,1)} async-done(((bf16[4,16,2048]{2,1,0:T(8,128)(2,1)}), bf16[256,16,2048]{2,1,0:T(8,128)(2,1)}) %all-gather.11.cloned.1.call-update) | async-done | bytes 16777232 | tf_op jit(solution)/shard_map/all_gather | solution.py:90
  455.8 23.4 %fusion.2 = bf16[4,16,2048]{2,0,1:T(4,128)(2,1)S(1)} fusion(bf16[256,16,2048]{2,1,0:T(8,128)(2,1)} %all-gather.11.cloned.1.call-done, s32[256]{0:T(256)S(1)} %copy-done.5, s32[4]{0:T(128)S(1)} %iota_add_fusion), kind=kOutput, calls=%fused_computation.2 | convolution fusion | flops 67240960 | bytes 17040400 | tf_op jit(solution)/shard_map/rs,sid->rid/dot_general | solution.py:87
  479.2 0.9 copy.78
  (32 shorter events, 0.7 us)
Async XLA Ops:
  6.5 123.2 %all-gather.7.cloned.1.call-start = ((), (), s32[]{:S(2)}) async-start(), calls=%async_computation.3 | async-start | bytes 4259840 | tf_op jit(solution)/shard_map/all_gather | solution.py:62
  7.3 238.4 %all-gather.9.cloned.1.call-start = ((), (), s32[]{:S(2)}) async-start(), calls=%async_computation.4 | async-start | bytes 4259840 | tf_op jit(solution)/shard_map/all_gather | solution.py:63
  136.2 116.0 %all-to-all-start = ((bf16[2048,4,256]{0,2,1:T(8,128)(2,1)}), bf16[2048,4,256]{0,2,1:T(8,128)(2,1)}, u32[]{:S(2)}, u32[]{:S(2)}) async-start(bf16[2048,4,256]{0,2,1:T(8,128)(2,1)} %bitcast.57), calls=%async_computation | async-start | bytes 8388608 | tf_op jit(solution)/shard_map/all_to_all | solution.py:66
  141.1 137.8 %all-gather.5.cloned.1.call-start = ((), (), s32[]{:S(2)}) async-start(), calls=%async_computation.2 | async-start | bytes 1310720 | tf_op jit(solution)/shard_map/all_gather | solution.py:59
  252.2 5.1 %copy-start.4 = (bf16[4,16,2048]{2,1,0:T(8,128)(2,1)S(1)}, bf16[4,16,2048]{2,1,0:T(8,128)(2,1)}, u32[]{:S(2)}) copy-start(bf16[4,16,2048]{2,1,0:T(8,128)(2,1)} %param.12) | copy-start | bytes 786436
  252.2 5.1 %copy-start.1 = (bf16[4,512,256]{2,1,0:T(8,128)(2,1)S(1)}, bf16[4,512,256]{2,1,0:T(8,128)(2,1)}, u32[]{:S(2)}) copy-start(bf16[4,512,256]{2,1,0:T(8,128)(2,1)} %param.13) | copy-start | bytes 3145732
  252.2 62.4 %all-to-all-start.1 = ((bf16[2048,4,256]{0,2,1:T(8,128)(2,1)}), bf16[2048,4,256]{0,2,1:T(8,128)(2,1)}, u32[]{:S(2)}, u32[]{:S(2)}) async-start(bf16[2048,4,256]{0,2,1:T(8,128)(2,1)} %bitcast.56), calls=%async_computation.1 | async-start | bytes 8388608 | tf_op jit(solution)/shard_map/all_to_all | solution.py:67
  257.2 1.4 copy-start.2
  257.2 198.6 %all-gather.11.cloned.1.call-start = ((), (), s32[]{:S(2)}) async-start(), calls=%async_computation.5 | async-start | bytes 17039360 | tf_op jit(solution)/shard_map/all_gather | solution.py:90
  257.3 1.6 copy-start.7
  257.3 1.6 copy-start.6
  320.8 2.7 copy-start
  323.5 1.2 copy-start.3
  324.8 131.0 %copy-start.5 = (s32[256]{0:T(256)S(1)}, s32[256]{0:T(256)}, u32[]{:S(2)}) copy-start(s32[256]{0:T(256)} %param.17) | copy-start | bytes 3076
Sparse Core Ops, SparseCore 0:
  9.2 120.4 all-gather.6
  131.5 114.0 all-gather.8
  247.5 31.4 all-gather.4
  326.6 129.1 all-gather.10
where the time goes:
time: 488 us; the launch traced here: 487 us
  waiting for transfers between devices  391 us (80%)
  local copies, waits for them, and re-layouts  37.7 us (8%)
  matrix products  31.1 us (6%)
  between operations  13.3 us (3%)
  starting transfers between devices  10 us (2%)
    all_gather x1, waiting for transfers between devices, shards(): lax.all_gather(attended, ('sect', 'dp'), axis=0, tiled=True)  129 us
    all_gather x1, waiting for transfers between devices, shards(): lax.all_gather(w_key, ('sect', 'dp'), axis=0, tiled=True)  122 us
    all_gather x1, waiting for transfers between devices, shards(): lax.all_gather(w_value, ('sect', 'dp'), axis=0, tiled=True)  104 us
    all_to_all x1, waiting for transfers between devices, shards(): lax.all_to_all(rows_value, 'tp', split_axis=1, concat_axis=0, tiled=True)  27.1 us
    dot_general x1, matrix products, shards(): jnp.einsum('rs,sid->rid', select, lax.all_gather(attended, ('sect', 'dp')...  23.4 us
  transfers between devices with their start and end apart: 6, of which 5 were waited for; matrix products, arithmetic and copies ran while one was open for 7% of the time, Pallas kernels for 0%

commit v1 on v0

v1 whole, which is shorter than its diff:
```python
import functools

import jax
import jax.numpy as jnp
from jax import lax
from jax.experimental import pallas as pl
from jax.experimental.pallas import tpu as pltpu
from jax.sharding import PartitionSpec as P

MESH = pl.DeviceIdType.MESH
HEAD = 128
STEPS = 16
CTX = 512
GROUP = 8
SEQ = 4
TOK = SEQ * STEPS
NX, NY, NZ = 4, 4, 8
HOLDERS = 64
LOG2E = 1.4426950408889634
NEG = -1e30


def kernel(
    lens, rolls, slots, w_key, w_value, hidden, queries, key_cache, value_cache, out,
    acts, weights, qs, kc, vc, part, part_send, part_recv, fresh, qrows, oc, mc, lc, pick,
    send_a, recv_a, send_b, recv_b, wide_a, wide_b,
    loc, w1s, w1r, h1s, h1r, ups, upr, dns, dnr, fus, fur, fds, fdr,
    zus, zur, zds, zdr, cs, cr, rs, rr, a_s, a_r, b_s, b_r,
):
    sect, dp, tp = lax.axis_index("sect"), lax.axis_index("dp"), lax.axis_index("tp")
    z_hi, x, core = dp // 8, (dp // 2) % 4, dp % 2
    z = 2 * z_hi + sect
    me = sect * 32 + dp

    def at_z(d):
        return (z + d + NZ) % NZ

    def block(zp):
        return (zp % 2) * 4 + zp // 2

    def device(dx=0, dy=0, dz=0, other=False):
        zp = at_z(dz)
        c = 1 - core if other else core
        return (zp % 2, (zp // 2) * 8 + ((x + dx + NX) % NX) * 2 + c, (tp + dy + NY) % NY)

    started = []

    def send(src, dst, s_sem, r_sem, to):
        copy = pltpu.make_async_remote_copy(
            src_ref=src, dst_ref=dst, send_sem=s_sem, recv_sem=r_sem, device_id=to, device_id_type=MESH
        )
        copy.start()
        started.append(copy)
        return copy

    def local(src, dst, sem):
        copy = pltpu.make_async_copy(src, dst, sem)
        copy.start()
        return copy

    zz = block(z)
    rows_w = pl.ds(pl.multiple_of(core * 128 + tp * 32, 32), 32)

    def cols(y):
        return pl.ds(pl.multiple_of(y * 256, 256), 256)

    w1 = []
    for k in range(1, NY):
        y = (tp + k) % NY
        w1.append(
            [
                send(w_key.at[:, cols(y)], weights.at[zz, rows_w, 0:256], w1s.at[k - 1, 0], w1r.at[k - 1, 0], device(dy=k)),
                send(w_value.at[:, cols(y)], weights.at[zz, rows_w, 256:512], w1s.at[k - 1, 1], w1r.at[k - 1, 1], device(dy=k)),
            ]
        )
    own_w = [
        local(w_key.at[:, cols(tp)], weights.at[zz, rows_w, 0:256], loc.at[0]),
        local(w_value.at[:, cols(tp)], weights.at[zz, rows_w, 256:512], loc.at[1]),
    ]
    my_rows = pl.ds(pl.multiple_of(x * TOK, TOK), TOK)

    def feats(half, xp):
        return pl.ds(pl.multiple_of(half * 1024 + xp * 256, 256), 256)

    h1 = {}
    for k in (1, 3, 2):
        to = (x + k) % NX
        h1[k] = [
            send(hidden.at[:, feats(b, to)], acts.at[tp, my_rows, b * 256 : b * 256 + 256], h1s.at[k - 1, b], h1r.at[k - 1, b], device(dx=k))
            for b in range(2)
        ]
    own_h = [
        local(hidden.at[:, feats(b, x)], acts.at[tp, my_rows, b * 256 : b * 256 + 256], loc.at[2 + b])
        for b in range(2)
    ]
    own_q = [local(queries, qs, loc.at[4]), local(key_cache, kc, loc.at[5]), local(value_cache, vc, loc.at[6])]

    def chunk(d, h):
        return weights.at[block(at_z(d)), pl.ds(pl.multiple_of(core * 128 + h * 64, 64), 64), :]

    up, down, across = {}, {}, []

    def zsend(step, h, direction):
        if direction > 0:
            ref = chunk(-(step - 1), h)
            up[step, h] = send(ref, ref, zus.at[step - 1, h], zur.at[step - 1, h], device(dz=1))
        else:
            ref = chunk(step - 1, h)
            down[step, h] = send(ref, ref, zds.at[step - 1, h], zdr.at[step - 1, h], device(dz=-1))

    def to_core(d, h):
        ref = chunk(d, h)
        across.append(send(ref, ref, cs.at[d % NZ, h], cr.at[d % NZ, h], device(other=True)))

    def zstep(step, h):
        up[step, h].wait_recv()
        if step < 3 or h == 0:
            zsend(step + 1, h, 1)
        down[step, h].wait_recv()
        if step < 3 or h == 1:
            zsend(step + 1, h, -1)
        to_core(-step, h)
        to_core(step, h)

    for pair in w1:
        for copy in pair:
            copy.wait_recv()
    for copy in own_w:
        copy.wait()
    for h in range(2):
        zsend(1, h, 1)
        zsend(1, h, -1)
    for h in range(2):
        to_core(0, h)

    def rows_of(k):
        return pl.ds(pl.multiple_of(((x - k + NX) % NX) * TOK, TOK), TOK)

    hup, hdn, hfu, hfd = {}, {}, {}, {}

    def ysend(k):
        ref = acts.at[tp, rows_of(k), :]
        hup[k] = send(ref, ref, ups.at[k], upr.at[k], device(dy=1))
        hdn[k] = send(ref, ref, dns.at[k], dnr.at[k], device(dy=-1))

    def yforward(k):
        if k % 2 == 0:
            hup[k].wait_recv()
            ref = acts.at[(tp + NY - 1) % NY, rows_of(k), :]
            hfu[k] = send(ref, ref, fus.at[k // 2], fur.at[k // 2], device(dy=1))
        else:
            hdn[k].wait_recv()
            ref = acts.at[(tp + 1) % NY, rows_of(k), :]
            hfd[k] = send(ref, ref, fds.at[k // 2], fdr.at[k // 2], device(dy=-1))

    for copy in own_h:
        copy.wait()
    ysend(0)
    for k in (1, 3, 2):
        for copy in h1[k]:
            copy.wait_recv()
        ysend(k)

    scale = HEAD ** (-0.5) * LOG2E

    def over_cache(n, kv):
        q = jnp.concatenate(
            [qs[n * STEPS : (n + 1) * STEPS, (kv * GROUP + g) * HEAD : (kv * GROUP + g + 1) * HEAD] for g in range(GROUP)],
            axis=0,
        )
        rows = slice(n * 128, (n + 1) * 128)
        qrows[kv, rows, :] = q
        keys = kc[n * CTX : (n + 1) * CTX, kv * HEAD : (kv + 1) * HEAD]
        vals = vc[n * CTX : (n + 1) * CTX, kv * HEAD : (kv + 1) * HEAD]
        score = lax.dot_general(q, keys, (((1,), (1,)), ((), ())), preferred_element_type=jnp.float32)
        live = lax.broadcasted_iota(jnp.int32, (128, CTX), 1) < lens[n]
        score = jnp.where(live, score * scale, NEG)
        top = jnp.max(score, axis=1, keepdims=True)
        e = jnp.exp2(score - top)
        total = jnp.sum(e, axis=1, keepdims=True)
        oc[kv, rows, :] = jnp.dot(e.astype(jnp.bfloat16), vals, preferred_element_type=jnp.float32)
        mc[kv, rows, :] = jnp.broadcast_to(top, (128, HEAD))
        lc[kv, rows, :] = jnp.broadcast_to(total, (128, HEAD))

    row = lax.broadcasted_iota(jnp.int32, (256, 256), 0)
    pick[...] = jnp.where(row == slots[...], 1.0, 0.0).astype(jnp.bfloat16)

    zstep(1, 0)
    yforward(0)
    zstep(1, 1)
    yforward(1)
    for copy in own_q:
        copy.wait()
    over_cache(0, 0)
    yforward(3)
    zstep(2, 0)
    yforward(2)
    over_cache(0, 1)
    zstep(2, 1)
    over_cache(1, 0)
    zstep(3, 0)
    over_cache(1, 1)
    zstep(3, 1)
    over_cache(2, 0)
    over_cache(2, 1)
    up[4, 0].wait_recv()
    to_core(4, 0)
    down[4, 1].wait_recv()
    to_core(4, 1)
    over_cache(3, 0)
    over_cache(3, 1)
    for k in (1, 3):
        hup[k].wait_recv()
    for k in (0, 2):
        hdn[k].wait_recv()
    for copy in list(hfu.values()) + list(hfd.values()) + across:
        copy.wait_recv()

    total = None
    for y in range(NY):
        term = jnp.dot(
            acts[y], weights[2 * y : 2 * y + 2].reshape(512, 512), preferred_element_type=jnp.float32
        )
        total = term if total is None else total + term
    part[...] = total.reshape(NX, TOK, 512)
    part_send[...] = total.reshape(NX, TOK, 512).astype(jnp.bfloat16)
    sums = [
        send(part_send.at[(x + k) % NX], part_recv.at[k - 1], rs.at[k - 1], rr.at[k - 1], device(dx=k))
        for k in (1, 3, 2)
    ]
    for copy in sums:
        copy.wait_recv()
    both = part[x]
    for k in range(3):
        both = both + part_recv[k].astype(jnp.float32)
    fresh[...] = both.astype(jnp.bfloat16)

    r = lax.broadcasted_iota(jnp.int32, (512, TOK), 0)
    j = lax.broadcasted_iota(jnp.int32, (512, TOK), 1)
    seen = (r // 128 == j // STEPS) & (j % STEPS <= r % STEPS)
    step = lax.broadcasted_iota(jnp.int32, (128, HEAD), 0) % STEPS
    for kv in range(2):
        keys = fresh[:, kv * HEAD : (kv + 1) * HEAD]
        vals = fresh[:, 256 + kv * HEAD : 256 + (kv + 1) * HEAD]
        score = lax.dot_general(qrows[kv], keys, (((1,), (1,)), ((), ())), preferred_element_type=jnp.float32)
        score = jnp.where(seen, score * scale, NEG)
        old = mc[kv]
        top = jnp.maximum(old, jnp.broadcast_to(jnp.max(score, axis=1, keepdims=True), (512, HEAD)))
        e = jnp.exp2(score - top[:, :TOK])
        shrink = jnp.exp2(old - top)
        denom = lc[kv] * shrink + jnp.broadcast_to(jnp.sum(e, axis=1, keepdims=True), (512, HEAD))
        value = oc[kv] * shrink + jnp.dot(e.astype(jnp.bfloat16), vals, preferred_element_type=jnp.float32)
        value = value / denom
        for n in range(SEQ):
            oc[kv, n * 128 : (n + 1) * 128, :] = jnp.where(step < rolls[n], value[n * 128 : (n + 1) * 128], 0.0)
        for q in range(32):
            send_a[kv * 32 + q] = oc[kv, pl.ds(q, 16, stride=32), :].astype(jnp.bfloat16)

    def spread(src, dst, s_sem, r_sem):
        def one(k, carry):
            to = (me + k) % HOLDERS
            pltpu.make_async_remote_copy(
                src_ref=src.at[to], dst_ref=dst.at[me], send_sem=s_sem, recv_sem=r_sem,
                device_id=(to // 32, to % 32, tp), device_id_type=MESH,
            ).start()
            return carry

        lax.fori_loop(1, HOLDERS, one, 0)
        dst[me] = src[me]

    def arrived(buf, sem):
        some = buf.at[pl.ds(0, HOLDERS - 1)]
        pltpu.make_async_copy(some, some, sem).wait()

    spread(send_a, recv_a, a_s, a_r)
    arrived(recv_a, a_r)
    wide_a[...] = recv_a[...].reshape(1024, HEAD).astype(jnp.float32)
    for u in range(4):
        pieces = wide_a[pl.ds(u, 256, stride=4), :].astype(jnp.bfloat16)
        wide_b[pl.ds(u, 256, stride=4), :] = jnp.dot(pick[...], pieces, preferred_element_type=jnp.float32)
    send_b[...] = wide_b[...].astype(jnp.bfloat16).reshape(HOLDERS, 16, HEAD)
    spread(send_b, recv_b, b_s, b_r)
    arrived(recv_b, b_r)
    wide_a[...] = recv_b[...].reshape(1024, HEAD).astype(jnp.float32)
    for kv in range(2):
        for qh in range(2):
            for u in range(4):
                col = (kv * GROUP + 2 * u + qh) * HEAD
                for n in range(SEQ):
                    base = (kv * 2 + qh) * 256 + n * 4 + u
                    out[n * STEPS : (n + 1) * STEPS, col : col + HEAD] = wide_a[
                        pl.ds(base, 16, stride=16), :
                    ].astype(jnp.bfloat16)
    for copy in started:
        copy.wait_send()
    arrived(send_a, a_s)
    arrived(send_b, b_s)


def shards(
    w_key, w_value, hidden, queries, key_cache, value_cache, prompt_lengths, rollout_lengths, batch_slots
):
    bf, f32 = jnp.bfloat16, jnp.float32
    vm, dma = pltpu.VMEM, pltpu.SemaphoreType.DMA
    hbm = pl.BlockSpec(memory_space=pl.ANY)
    smem = pl.BlockSpec(memory_space=pltpu.SMEM)
    vmem = pl.BlockSpec(memory_space=pltpu.VMEM)
    scratch = [
        vm((NY, NX * TOK, 512), bf),
        vm((NZ, 256, 512), bf),
        vm((TOK, 2048), bf),
        vm((SEQ * CTX, 256), bf),
        vm((SEQ * CTX, 256), bf),
        vm((NX, TOK, 512), f32),
        vm((NX, TOK, 512), bf),
        vm((NX - 1, TOK, 512), bf),
        vm((TOK, 512), bf),
        vm((2, 512, HEAD), bf),
        vm((2, 512, HEAD), f32),
        vm((2, 512, HEAD), f32),
        vm((2, 512, HEAD), f32),
        vm((256, 256), bf),
    ]
    scratch += [vm((HOLDERS, 16, HEAD), bf)] * 4 + [vm((1024, HEAD), f32)] * 2
    scratch += [dma((7,))]
    scratch += [dma((3, 2))] * 4
    scratch += [dma((4,))] * 4 + [dma((2,))] * 4
    scratch += [dma((4, 2))] * 4 + [dma((NZ, 2))] * 2
    scratch += [dma((3,))] * 2
    scratch += [dma] * 4
    result = pl.pallas_call(
        kernel,
        out_shape=jax.ShapeDtypeStruct((TOK, 2048), bf),
        in_specs=[smem, smem, vmem] + [hbm] * 6,
        out_specs=vmem,
        scratch_shapes=scratch,
        compiler_params=pltpu.CompilerParams(has_side_effects=True, vmem_limit_bytes=32 * 1024 * 1024),
        name="rollout",
    )(
        prompt_lengths,
        rollout_lengths,
        batch_slots.reshape(1, 256),
        w_key,
        w_value,
        hidden.reshape(TOK, 2048),
        queries.reshape(TOK, 2048),
        key_cache.reshape(SEQ * CTX, 256),
        value_cache.reshape(SEQ * CTX, 256),
    )
    return result.reshape(SEQ, STEPS, 2048)


def solution(mesh):
    rows = P(("sect", "dp", "tp"), None)
    spread = P(("sect", "dp"), None, "tp")
    each = P(("sect", "dp"))
    return jax.shard_map(
        shards,
        mesh=mesh,
        in_specs=(rows, rows, spread, spread, spread, spread, each, each, P()),
        out_specs=spread,
        check_vma=False,
    )
```

time: 488 us -> 76.5 us (0.16)
  waiting for transfers between devices: 391 us -> 0 us
  Pallas kernels: 0 us -> 68.8 us
  matrix products: 31.1 us -> 0 us
  local copies, waits for them, and re-layouts: 37.7 us -> 7.42 us
  between operations: 13.3 us -> 0.02 us
  starting transfers between devices: 10 us -> 0 us
    all_gather x4 -> x0, waiting for transfers between devices: 362 us -> none  [the longest x1 129 us: shards(): lax.all_gather(attended, ('sect', 'dp'), axis=0, tiled=True)]
    pallas_call x0 -> x1, Pallas kernels: none -> 68.8 us  [shards(): pl.pallas_call(kernel, out_shape=jax.ShapeDtypeStruct((TOK, 2048), bf), i...]
    dot_general x7 -> x0, matrix products: 31.1 us -> none  [the longest x1 23.4 us: shards(): jnp.einsum('rs,sid->rid', select, lax.all_gather(attended, ('sect', 'dp')...]
    all_to_all x2 -> x0, waiting for transfers between devices: 27.1 us -> none  [the longest x1 27.1 us: shards(): lax.all_to_all(rows_value, 'tp', split_axis=1, concat_axis=0, tiled=True)]
    all_gather x2 -> x0, local copies, waits for them, and re-layouts: 13 us -> none  [the longest x1 6.54 us: shards(): lax.all_gather(w_value, ('sect', 'dp'), axis=0, tiled=True)]
    all_to_all x2 -> x0, local copies, waits for them, and re-layouts: 12.5 us -> none  [the longest x1 6.25 us: shards(): lax.all_to_all(rows_key, 'tp', split_axis=1, concat_axis=0, tiled=True)]
    all_to_all x2 -> x0, starting transfers between devices: 9.92 us -> none  [the longest x1 4.98 us: shards(): lax.all_to_all(rows_value, 'tp', split_axis=1, concat_axis=0, tiled=True)]
    transpose x2 -> x0, local copies, waits for them, and re-layouts: 7.53 us -> none  [reorder(): a.reshape(heads_tp, groups, block, width).transpose(1, 0, 2, 3)]
  transfers between devices with their start and end apart: 6 -> 0, of which waited for: 5 -> 0; matrix products, arithmetic and copies ran while one was open for 7% -> 0% of each run, Pallas kernels for 0% -> 0%
where the time goes in v1:
time: 76.5 us; the launch traced here: 76.2 us
  Pallas kernels  68.8 us (90%)
  local copies, waits for them, and re-layouts  7.42 us (10%)
    pallas_call x1, Pallas kernels, shards(): pl.pallas_call(kernel, out_shape=jax.ShapeDtypeStruct((TOK, 2048), bf), i...  68.8 us
    unnamed x19, local copies, waits for them, and re-layouts  7.42 us

profile of v1, /device:TPU:1, one launch (start us, length us, event | category | flops | bytes accessed | tf_op | source)
XLA Modules:
  0.0 76.2 jit_solution(18121157570628746095)
XLA Ops:
  0.0 0.0 copy-start.8
  0.0 0.0 copy-start.6
  0.0 0.0 copy-start.7
  0.0 0.6 copy-done.8
  0.7 0.0 copy-done.6
  0.7 0.0 copy-done.7
  0.7 0.0 copy-start
  0.7 1.2 %copy-done = bf16[4,512,256]{2,1,0:T(8,128)(2,1)S(1)} copy-done((bf16[4,512,256]{2,1,0:T(8,128)(2,1)S(1)}, bf16[4,512,256]{2,1,0:T(8,128)(2,1)}, u32[]{:S(2)}) %copy-start) | copy-done | bytes 1048600
  1.9 0.0 copy-start.1
  1.9 1.2 %copy-done.1 = bf16[4,512,256]{2,1,0:T(8,128)(2,1)S(1)} copy-done((bf16[4,512,256]{2,1,0:T(8,128)(2,1)S(1)}, bf16[4,512,256]{2,1,0:T(8,128)(2,1)}, u32[]{:S(2)}) %copy-start.1) | copy-done | bytes 1048600
  3.1 0.0 copy-start.2
  3.2 0.9 %copy-done.2 = bf16[4,16,2048]{2,1,0:T(8,128)(2,1)S(1)} copy-done((bf16[4,16,2048]{2,1,0:T(8,128)(2,1)S(1)}, bf16[4,16,2048]{2,1,0:T(8,128)(2,1)}, u32[]{:S(2)}) %copy-start.2) | copy-done | bytes 262168
  4.1 0.0 copy-start.3
  4.1 0.9 %copy-done.3 = bf16[4,16,2048]{2,1,0:T(8,128)(2,1)S(1)} copy-done((bf16[4,16,2048]{2,1,0:T(8,128)(2,1)S(1)}, bf16[4,16,2048]{2,1,0:T(8,128)(2,1)}, u32[]{:S(2)}) %copy-start.3) | copy-done | bytes 262168
  5.1 0.0 copy-start.4
  5.1 0.8 %copy-done.4 = bf16[32,1024]{1,0:T(8,128)(2,1)S(1)} copy-done((bf16[32,1024]{1,0:T(8,128)(2,1)S(1)}, bf16[32,1024]{1,0:T(8,128)(2,1)}, u32[]{:S(2)}) %copy-start.4) | copy-done | bytes 65560
  5.9 0.0 copy-start.5
  5.9 0.8 %copy-done.5 = bf16[32,1024]{1,0:T(8,128)(2,1)S(1)} copy-done((bf16[32,1024]{1,0:T(8,128)(2,1)S(1)}, bf16[32,1024]{1,0:T(8,128)(2,1)}, u32[]{:S(2)}) %copy-start.5) | copy-done | bytes 65560
  6.7 68.8 %rollout.1 = bf16[64,2048]{1,0:T(8,128)(2,1)S(1)} custom-call(s32[4]{0:T(128)S(1)} %copy-done.7, s32[4]{0:T(128)S(1)} %copy-done.8, s32[1,256]{1,0:T(1,128)S(1)} %bitcast.11, bf16[32,1024]{1,0:T(8,128)(2,1)S(1)} %copy-done.4, bf16[32,1024]{1,0:T(8,128)(2,1)S(1)} %copy-done.5, bf16[64,2048]{1,0:T(8,128)(2,1)S(1)} %bitcast.9, bf16[64,2048]{1,0:T(8,128)(2,1)S(1)} %bitcast.10, ...), custom_call_target="tpu_custom_call" | custom-call | tf_op jit(solution)/shard_map/rollout/pallas_call | solution.py:331
  75.5 0.7 copy.11
Async XLA Ops:
  0.0 0.7 copy-start.8
  0.0 0.7 copy-start.6
  0.0 0.7 copy-start.7
  0.7 1.2 %copy-start = (bf16[4,512,256]{2,1,0:T(8,128)(2,1)S(1)}, bf16[4,512,256]{2,1,0:T(8,128)(2,1)}, u32[]{:S(2)}) copy-start(bf16[4,512,256]{2,1,0:T(8,128)(2,1)} %param.13) | copy-start | bytes 3145732
  1.9 1.2 %copy-start.1 = (bf16[4,512,256]{2,1,0:T(8,128)(2,1)S(1)}, bf16[4,512,256]{2,1,0:T(8,128)(2,1)}, u32[]{:S(2)}) copy-start(bf16[4,512,256]{2,1,0:T(8,128)(2,1)} %param.14) | copy-start | bytes 3145732
  3.1 0.9 %copy-start.2 = (bf16[4,16,2048]{2,1,0:T(8,128)(2,1)S(1)}, bf16[4,16,2048]{2,1,0:T(8,128)(2,1)}, u32[]{:S(2)}) copy-start(bf16[4,16,2048]{2,1,0:T(8,128)(2,1)} %param.11) | copy-start | bytes 786436
  4.1 0.9 %copy-start.3 = (bf16[4,16,2048]{2,1,0:T(8,128)(2,1)S(1)}, bf16[4,16,2048]{2,1,0:T(8,128)(2,1)}, u32[]{:S(2)}) copy-start(bf16[4,16,2048]{2,1,0:T(8,128)(2,1)} %param.12) | copy-start | bytes 786436
  5.1 0.8 %copy-start.4 = (bf16[32,1024]{1,0:T(8,128)(2,1)S(1)}, bf16[32,1024]{1,0:T(8,128)(2,1)}, u32[]{:S(2)}) copy-start(bf16[32,1024]{1,0:T(8,128)(2,1)} %w_key.1) | copy-start | bytes 196612
  5.9 0.8 %copy-start.5 = (bf16[32,1024]{1,0:T(8,128)(2,1)S(1)}, bf16[32,1024]{1,0:T(8,128)(2,1)}, u32[]{:S(2)}) copy-start(bf16[32,1024]{1,0:T(8,128)(2,1)} %w_value.1) | copy-start | bytes 196612

commit v2 on v1

--- a/solution.py
+++ b/solution.py
@@ -42,6 +42,13 @@
         zp = at_z(dz)
         c = 1 - core if other else core
         return (zp % 2, (zp // 2) * 8 + ((x + dx + NX) % NX) * 2 + c, (tp + dy + NY) % NY)
+
+    partners = [device(dx=k) for k in range(1, NX)] + [device(dy=k) for k in range(1, NY)]
+    partners += [device(dz=1), device(dz=-1), device(other=True)]
+    barrier = pltpu.get_barrier_semaphore()
+    for partner in partners:
+        pl.semaphore_signal(barrier, inc=1, device_id=partner, device_id_type=MESH)
+    pl.semaphore_wait(barrier, len(partners))
 
     started = []
 
@@ -334,7 +341,7 @@
         in_specs=[smem, smem, vmem] + [hbm] * 6,
         out_specs=vmem,
         scratch_shapes=scratch,
-        compiler_params=pltpu.CompilerParams(has_side_effects=True, vmem_limit_bytes=32 * 1024 * 1024),
+        compiler_params=pltpu.CompilerParams(collective_id=0, has_side_effects=True, vmem_limit_bytes=60 * 1024 * 1024),
         name="rollout",
     )(
         prompt_lengths,

time: 76.5 us -> 62.6 us (0.82)
  Pallas kernels: 68.8 us -> 60.8 us
  local copies, waits for them, and re-layouts: 7.42 us -> 1.67 us
    pallas_call x1, Pallas kernels: 68.8 us -> 60.8 us  [shards(): pl.pallas_call(kernel, out_shape=jax.ShapeDtypeStruct((TOK, 2048), bf), i...]
    unnamed x19 -> x1, local copies, waits for them, and re-layouts: 7.42 us -> 1.67 us
where the time goes in v2:
time: 62.6 us; the launch traced here: 62.5 us
  Pallas kernels  60.8 us (97%)
  local copies, waits for them, and re-layouts  1.67 us (3%)
    pallas_call x1, Pallas kernels, shards(): pl.pallas_call(kernel, out_shape=jax.ShapeDtypeStruct((TOK, 2048), bf), i...  60.8 us
    unnamed x1, local copies, waits for them, and re-layouts  1.67 us

profile of v2, /device:TPU:1, one launch (start us, length us, event | category | flops | bytes accessed | tf_op | source)
XLA Modules:
  0.0 62.5 jit_solution(17026647457488860451)
XLA Ops:
  0.0 60.8 %rollout.1 = bf16[64,2048]{1,0:T(8,128)(2,1)} custom-call(s32[4]{0:T(128)} %lens.1, s32[4]{0:T(128)} %rolls.1, s32[1,256]{1,0:T(1,128)} %bitcast.11, bf16[32,1024]{1,0:T(8,128)(2,1)} %w_key.1, bf16[32,1024]{1,0:T(8,128)(2,1)} %w_value.1, bf16[64,2048]{1,0:T(8,128)(2,1)} %bitcast.9, bf16[64,2048]{1,0:T(8,128)(2,1)} %bitcast.10, bf16[2048,256]{1,0:T(8,128)(2,1)} %bitcast.7, ...), custom_call_target="tpu_custom_call" | custom-call | tf_op jit(solution)/shard_map/rollout/pallas_call | solution.py:338
  60.8 1.7 %copy.11 = bf16[4,16,2048]{2,1,0:T(8,128)(2,1)} copy(bf16[4,16,2048]{2,1,0:T(8,128)(2,1)} %bitcast.6) | data formatting | bytes 524288

commit v3 on v1

v3 whole, which is shorter than its diff:
```python
import functools

import jax
import jax.numpy as jnp
from jax import lax
from jax.experimental import pallas as pl
from jax.experimental.pallas import tpu as pltpu
from jax.sharding import PartitionSpec as P

MESH = pl.DeviceIdType.MESH
HEAD = 128
STEPS = 16
CTX = 512
GROUP = 8
SEQ = 4
TOK = SEQ * STEPS
NX, NY, NZ = 4, 4, 8
HOLDERS = 64
LOG2E = 1.4426950408889634
NEG = -1e30
FIRST = [(1,), (1,), (1,), (1,)]
ONWARD = [{1: (1,), 2: (1, 2)}] * 4
GREET = (-1, 1)


def kernel(
    lens, rolls, slots, w_key, w_value, hidden, queries, key_cache, value_cache, out,
    w_stage, h_stage, acts, weights, qs, kc, vc, part, part_send, part_recv, fresh, qrows, oc, mc, lc, pick,
    send_a, recv_a, send_b, recv_b, wide_a, wide_b,
    loc, w1s, w1r, h1s, h1r, ups, upr, dns, dnr, fus, fur, fds, fdr, hxs, hxr,
    zus, zur, zds, zdr, rs, rr, a_s, a_r, b_s, b_r,
):
    sect, dp, tp = lax.axis_index("sect"), lax.axis_index("dp"), lax.axis_index("tp")
    z_hi, x, core = dp // 8, (dp // 2) % 4, dp % 2
    z = 2 * z_hi + sect
    me = sect * 32 + dp

    def at_z(d):
        return (z + d + NZ) % NZ

    def block(zp):
        return (zp % 2) * 4 + zp // 2

    def device(dx=0, dy=0, dz=0, other=False):
        zp = at_z(dz)
        c = 1 - core if other else core
        return (zp % 2, (zp // 2) * 8 + ((x + dx + NX) % NX) * 2 + c, (tp + dy + NY) % NY)

    started = []

    def send(src, dst, s_sem, r_sem, to):
        copy = pltpu.make_async_remote_copy(
            src_ref=src, dst_ref=dst, send_sem=s_sem, recv_sem=r_sem, device_id=to, device_id_type=MESH
        )
        copy.start()
        started.append(copy)
        return copy

    def local(src, dst, sem):
        copy = pltpu.make_async_copy(src, dst, sem)
        copy.start()
        return copy

    zz = block(z)
    rows_w = pl.ds(pl.multiple_of(tp * 32, 32), 32)
    there = 1 - core

    def tokens(xp, c):
        return pl.ds(pl.multiple_of((c * NX + xp) * TOK, TOK), TOK)

    partners = [device(dx=k, other=o) for k in range(1, NX) for o in (False, True)]
    partners += [device(dy=k, other=o) for k in range(1, NY) for o in (False, True)] + [device(other=True)]
    partners += [device(dz=k) for k in GREET]
    barrier = pltpu.get_barrier_semaphore()
    for partner in partners:
        pl.semaphore_signal(barrier, inc=1, device_id=partner, device_id_type=MESH)
    own_q = [local(queries, qs, loc.at[0]), local(key_cache, kc, loc.at[1]), local(value_cache, vc, loc.at[2])]
    staged = [
        local(src.at[:, y * 256 : y * 256 + 256], w_stage.at[y, b], loc.at[3 + y * 2 + b])
        for y in range(NY)
        for b, src in enumerate((w_key, w_value))
    ]
    staged += [
        local(
            hidden.at[:, b * 1024 + xp * 256 : b * 1024 + xp * 256 + 256],
            h_stage.at[xp, :, b * 256 : b * 256 + 256],
            loc.at[11 + xp * 2 + b],
        )
        for xp in range(NX)
        for b in range(2)
    ]
    pl.semaphore_wait(barrier, len(partners))
    for copy in staged:
        copy.wait()

    w1 = {}

    def wsend(k, o):
        w1[k, o] = send(
            w_stage.at[(tp + k) % NY, there if o else core], weights.at[zz, core, rows_w, :],
            w1s.at[k, o], w1r.at[k, o], device(dy=k, other=o == 1),
        )

    up, down = {}, {}

    def piece(d, k):
        rows = pl.ds(pl.multiple_of(((tp - k + NY) % NY) * 32, 32), 32)
        return weights.at[block(at_z(d)), :, rows, :]

    def zsend(k, dist, hop=1):
        if dist < 4 or k < 2:
            ref = piece(hop - dist, k)
            up[k, dist] = [send(ref, ref, zus.at[k, dist - 1], zur.at[k, dist - 1], device(dz=hop))]
        if dist < 4 or k >= 2:
            ref = piece(dist - hop, k)
            down[k, dist] = [send(ref, ref, zds.at[k, dist - 1], zdr.at[k, dist - 1], device(dz=-hop))]

    def zfirst(k):
        for dist in FIRST[k]:
            zsend(k, dist, dist)

    def zpass(k, dist):
        for copy in up.get((k, dist), []) + down.get((k, dist), []):
            copy.wait_recv()
        for hop in ONWARD[k].get(dist, ()):
            zsend(k, dist + hop, hop)

    h1 = {}

    def hsend(k):
        h1[k] = send(
            h_stage.at[(x + k) % NX], acts.at[tp, tokens(x, core), :], h1s.at[k - 1], h1r.at[k - 1], device(dx=k)
        )

    hup, hdn, hfu, hfd, hx = {}, {}, {}, {}, {}

    def chunk(dy, k):
        return acts.at[(tp + dy + NY) % NY, tokens((x - k + NX) % NX, core), :]

    def hcore(dy, k):
        ref = chunk(dy, k)
        hx[dy, k] = send(ref, ref, hxs.at[dy % NY, k], hxr.at[dy % NY, k], device(other=True))

    def ysend(k):
        ref = chunk(0, k)
        hup[k] = send(ref, ref, ups.at[k], upr.at[k], device(dy=1))
        hdn[k] = send(ref, ref, dns.at[k], dnr.at[k], device(dy=-1))
        hcore(0, k)

    def yforward(k):
        if k % 2 == 0:
            hup[k].wait_recv()
            ref = chunk(-1, k)
            hfu[k] = send(ref, ref, fus.at[k // 2], fur.at[k // 2], device(dy=1))
            hcore(-1, k)
        else:
            hdn[k].wait_recv()
            ref = chunk(1, k)
            hfd[k] = send(ref, ref, fds.at[k // 2], fdr.at[k // 2], device(dy=-1))
            hcore(1, k)

    def yother(k):
        if k % 2 == 0:
            hdn[k].wait_recv()
            hcore(1, k)
        else:
            hup[k].wait_recv()
            hcore(-1, k)

    def ylast(k):
        (hfu if k % 2 == 0 else hfd)[k].wait_recv()
        hcore(2, k)

    for k in (2, 1, 3, 0):
        for o in range(2):
            if k or o:
                wsend(k, o)
    own = [local(w_stage.at[tp, core], weights.at[zz, core, rows_w, :], loc.at[19])]
    own += [local(h_stage.at[x], acts.at[tp, tokens(x, core), :], loc.at[20])]
    for k in (2, 1, 3):
        hsend(k)
    own[1].wait()
    ysend(0)
    own[0].wait()
    w1[0, 1].wait_recv()
    zfirst(0)

    scale = HEAD ** (-0.5) * LOG2E

    def over_cache(n, kv):
        q = jnp.concatenate(
            [qs[n * STEPS : (n + 1) * STEPS, (kv * GROUP + g) * HEAD : (kv * GROUP + g + 1) * HEAD] for g in range(GROUP)],
            axis=0,
        )
        rows = slice(n * 128, (n + 1) * 128)
        qrows[kv, rows, :] = q
        keys = kc[n * CTX : (n + 1) * CTX, kv * HEAD : (kv + 1) * HEAD]
        vals = vc[n * CTX : (n + 1) * CTX, kv * HEAD : (kv + 1) * HEAD]
        score = lax.dot_general(q, keys, (((1,), (1,)), ((), ())), preferred_element_type=jnp.float32)
        live = lax.broadcasted_iota(jnp.int32, (128, CTX), 1) < lens[n]
        score = jnp.where(live, score * scale, NEG)
        top = jnp.max(score, axis=1, keepdims=True)
        e = jnp.exp2(score - top)
        total = jnp.sum(e, axis=1, keepdims=True)
        oc[kv, rows, :] = jnp.dot(e.astype(jnp.bfloat16), vals, preferred_element_type=jnp.float32)
        mc[kv, rows, :] = jnp.broadcast_to(top, (128, HEAD))
        lc[kv, rows, :] = jnp.broadcast_to(total, (128, HEAD))

    row = lax.broadcasted_iota(jnp.int32, (256, 256), 0)
    pick[...] = jnp.where(row == slots[...], 1.0, 0.0).astype(jnp.bfloat16)

    for copy in own_q:
        copy.wait()
    over_cache(0, 0)

    def wfirst(k):
        for o in range(2):
            w1[k, o].wait_recv()
        zfirst(k)

    def hfirst(k):
        h1[k].wait_recv()
        ysend(k)

    over_cache(0, 1)
    wfirst(1)
    wfirst(3)
    zpass(0, 1)
    wfirst(2)
    hfirst(1)
    hfirst(3)
    yforward(0)
    hfirst(2)
    zpass(1, 1)
    zpass(3, 1)
    yother(0)
    zpass(0, 2)
    zpass(2, 1)
    yforward(1)
    yforward(3)
    yforward(2)
    zpass(1, 2)
    zpass(3, 2)
    for k in (1, 3, 2):
        yother(k)
    zpass(0, 3)
    zpass(2, 2)
    for k in (0, 1, 3, 2):
        ylast(k)
    zpass(0, 4)
    for k in (1, 3, 2):
        zpass(k, 3)
        zpass(k, 4)
    for copy in hx.values():
        copy.wait_recv()

    total = None
    for y in range(NY):
        term = jnp.dot(
            acts[y], weights[2 * y : 2 * y + 2].reshape(512, 256), preferred_element_type=jnp.float32
        )
        total = term if total is None else total + term
    part[...] = total.reshape(2, NX, TOK, 256)
    part_send[...] = total.reshape(2, NX, TOK, 256).astype(jnp.bfloat16)
    sums = [
        send(
            part_send.at[there if o else core, (x + k) % NX], part_recv.at[o, k],
            rs.at[o, k], rr.at[o, k], device(dx=k, other=o == 1),
        )
        for k in (2, 1, 3, 0)
        for o in range(2)
        if k or o
    ]
    over_cache(1, 0)
    over_cache(1, 1)
    over_cache(2, 0)
    over_cache(2, 1)
    over_cache(3, 0)
    over_cache(3, 1)
    for copy in sums:
        copy.wait_recv()
    same, cross = part[core, x], part_recv[1, 0].astype(jnp.float32)
    for k in range(1, NX):
        same = same + part_recv[0, k].astype(jnp.float32)
        cross = cross + part_recv[1, k].astype(jnp.float32)
    fresh[core] = same.astype(jnp.bfloat16)
    fresh[there] = cross.astype(jnp.bfloat16)

    r = lax.broadcasted_iota(jnp.int32, (512, TOK), 0)
    j = lax.broadcasted_iota(jnp.int32, (512, TOK), 1)
    seen = (r // 128 == j // STEPS) & (j % STEPS <= r % STEPS)
    step = lax.broadcasted_iota(jnp.int32, (128, HEAD), 0) % STEPS
    for kv in range(2):
        keys = fresh[0, :, kv * HEAD : (kv + 1) * HEAD]
        vals = fresh[1, :, kv * HEAD : (kv + 1) * HEAD]
        score = lax.dot_general(qrows[kv], keys, (((1,), (1,)), ((), ())), preferred_element_type=jnp.float32)
        score = jnp.where(seen, score * scale, NEG)
        old = mc[kv]
        top = jnp.maximum(old, jnp.broadcast_to(jnp.max(score, axis=1, keepdims=True), (512, HEAD)))
        e = jnp.exp2(score - top[:, :TOK])
        shrink = jnp.exp2(old - top)
        denom = lc[kv] * shrink + jnp.broadcast_to(jnp.sum(e, axis=1, keepdims=True), (512, HEAD))
        value = oc[kv] * shrink + jnp.dot(e.astype(jnp.bfloat16), vals, preferred_element_type=jnp.float32)
        value = value / denom
        for n in range(SEQ):
            oc[kv, n * 128 : (n + 1) * 128, :] = jnp.where(step < rolls[n], value[n * 128 : (n + 1) * 128], 0.0)
        for q in range(32):
            send_a[kv * 32 + q] = oc[kv, pl.ds(q, 16, stride=32), :].astype(jnp.bfloat16)

    def spread(src, dst, s_sem, r_sem):
        for dx in (2, 1, 3, 0):
            for dz in (4, 3, 5, 2, 6, 1, 7, 0):
                for o in (False, True):
                    if dz or dx or o:
                        to = device(dx=dx, dz=dz, other=o)
                        pltpu.make_async_remote_copy(
                            src_ref=src.at[to[0] * 32 + to[1]], dst_ref=dst.at[me], send_sem=s_sem, recv_sem=r_sem,
                            device_id=to, device_id_type=MESH,
                        ).start()
        dst[me] = src[me]

    def arrived(buf, sem):
        some = buf.at[pl.ds(0, HOLDERS - 1)]
        pltpu.make_async_copy(some, some, sem).wait()

    spread(send_a, recv_a, a_s, a_r)
    arrived(recv_a, a_r)
    wide_a[...] = recv_a[...].reshape(1024, HEAD).astype(jnp.float32)
    for u in range(4):
        pieces = wide_a[pl.ds(u, 256, stride=4), :].astype(jnp.bfloat16)
        wide_b[pl.ds(u, 256, stride=4), :] = jnp.dot(pick[...], pieces, preferred_element_type=jnp.float32)
    send_b[...] = wide_b[...].astype(jnp.bfloat16).reshape(HOLDERS, 16, HEAD)
    spread(send_b, recv_b, b_s, b_r)
    arrived(recv_b, b_r)
    wide_a[...] = recv_b[...].reshape(1024, HEAD).astype(jnp.float32)
    for kv in range(2):
        for qh in range(2):
            for u in range(4):
                col = (kv * GROUP + 2 * u + qh) * HEAD
                for n in range(SEQ):
                    base = (kv * 2 + qh) * 256 + n * 4 + u
                    out[n * STEPS : (n + 1) * STEPS, col : col + HEAD] = wide_a[
                        pl.ds(base, 16, stride=16), :
                    ].astype(jnp.bfloat16)
    for copy in started:
        copy.wait_send()
    arrived(send_a, a_s)
    arrived(send_b, b_s)


def shards(
    w_key, w_value, hidden, queries, key_cache, value_cache, prompt_lengths, rollout_lengths, batch_slots
):
    bf, f32 = jnp.bfloat16, jnp.float32
    vm, dma = pltpu.VMEM, pltpu.SemaphoreType.DMA
    hbm = pl.BlockSpec(memory_space=pl.ANY)
    smem = pl.BlockSpec(memory_space=pltpu.SMEM)
    vmem = pl.BlockSpec(memory_space=pltpu.VMEM)
    scratch = [
        vm((NY, 2, 32, 256), bf),
        vm((NX, TOK, 512), bf),
        vm((NY, 2 * NX * TOK, 512), bf),
        vm((NZ, 2, 128, 256), bf),
        vm((TOK, 2048), bf),
        vm((SEQ * CTX, 256), bf),
        vm((SEQ * CTX, 256), bf),
        vm((2, NX, TOK, 256), f32),
        vm((2, NX, TOK, 256), bf),
        vm((2, NX, TOK, 256), bf),
        vm((2, TOK, 256), bf),
        vm((2, 512, HEAD), bf),
        vm((2, 512, HEAD), f32),
        vm((2, 512, HEAD), f32),
        vm((2, 512, HEAD), f32),
        vm((256, 256), bf),
    ]
    scratch += [vm((HOLDERS, 16, HEAD), bf)] * 4 + [vm((1024, HEAD), f32)] * 2
    scratch += [dma((21,))]
    scratch += [dma((4, 2))] * 2 + [dma((3,))] * 2
    scratch += [dma((4,))] * 4 + [dma((2,))] * 4 + [dma((4, 4))] * 2
    scratch += [dma((4, 4))] * 4
    scratch += [dma((2, 4))] * 2
    scratch += [dma] * 4
    result = pl.pallas_call(
        kernel,
        out_shape=jax.ShapeDtypeStruct((TOK, 2048), bf),
        in_specs=[smem, smem, vmem] + [hbm] * 6,
        out_specs=vmem,
        scratch_shapes=scratch,
        compiler_params=pltpu.CompilerParams(collective_id=0, has_side_effects=True, vmem_limit_bytes=60 * 1024 * 1024),
        name="rollout",
    )(
        prompt_lengths,
        rollout_lengths,
        batch_slots.reshape(1, 256),
        w_key,
        w_value,
        hidden.reshape(TOK, 2048),
        queries.reshape(TOK, 2048),
        key_cache.reshape(SEQ * CTX, 256),
        value_cache.reshape(SEQ * CTX, 256),
    )
    return result.reshape(SEQ, STEPS, 2048)


def solution(mesh):
    rows = P(("sect", "dp", "tp"), None)
    spread = P(("sect", "dp"), None, "tp")
    each = P(("sect", "dp"))
    return jax.shard_map(
        shards,
        mesh=mesh,
        in_specs=(rows, rows, spread, spread, spread, spread, each, each, P()),
        out_specs=spread,
        check_vma=False,
    )
```

time: 76.5 us -> 58.7 us (0.77)
  Pallas kernels: 68.8 us -> 56.9 us
  local copies, waits for them, and re-layouts: 7.42 us -> 1.67 us
    pallas_call x1, Pallas kernels: 68.8 us -> 56.9 us  [shards(): pl.pallas_call(kernel, out_shape=jax.ShapeDtypeStruct((TOK, 2048), bf), i...]
    unnamed x19 -> x1, local copies, waits for them, and re-layouts: 7.42 us -> 1.67 us
where the time goes in v3:
time: 58.7 us; the launch traced here: 58.5 us
  Pallas kernels  56.9 us (97%)
  local copies, waits for them, and re-layouts  1.67 us (3%)
    pallas_call x1, Pallas kernels, shards(): pl.pallas_call(kernel, out_shape=jax.ShapeDtypeStruct((TOK, 2048), bf), i...  56.9 us
    unnamed x1, local copies, waits for them, and re-layouts  1.67 us

profile of v3, /device:TPU:1, one launch (start us, length us, event | category | flops | bytes accessed | tf_op | source)
XLA Modules:
  0.0 58.5 jit_solution(13242909189675655052)
XLA Ops:
  0.0 56.9 %rollout.1 = bf16[64,2048]{1,0:T(8,128)(2,1)} custom-call(s32[4]{0:T(128)} %lens.1, s32[4]{0:T(128)} %rolls.1, s32[1,256]{1,0:T(1,128)} %bitcast.11, bf16[32,1024]{1,0:T(8,128)(2,1)} %w_key.1, bf16[32,1024]{1,0:T(8,128)(2,1)} %w_value.1, bf16[64,2048]{1,0:T(8,128)(2,1)} %bitcast.9, bf16[64,2048]{1,0:T(8,128)(2,1)} %bitcast.10, bf16[2048,256]{1,0:T(8,128)(2,1)} %bitcast.7, ...), custom_call_target="tpu_custom_call" | custom-call | tf_op jit(solution)/shard_map/rollout/pallas_call | solution.py:384
  56.9 1.7 %copy.11 = bf16[4,16,2048]{2,1,0:T(8,128)(2,1)} copy(bf16[4,16,2048]{2,1,0:T(8,128)(2,1)} %bitcast.6) | data formatting | bytes 524288

commit v4 on v3

--- a/solution.py
+++ b/solution.py
@@ -21,14 +21,15 @@
 FIRST = [(1,), (1,), (1,), (1,)]
 ONWARD = [{1: (1,), 2: (1, 2)}] * 4
 GREET = (-1, 1)
+STRAIGHT = ()
 
 
 def kernel(
     lens, rolls, slots, w_key, w_value, hidden, queries, key_cache, value_cache, out,
     w_stage, h_stage, acts, weights, qs, kc, vc, part, part_send, part_recv, fresh, qrows, oc, mc, lc, pick,
-    send_a, recv_a, send_b, recv_b, wide_a, wide_b,
-    loc, w1s, w1r, h1s, h1r, ups, upr, dns, dnr, fus, fur, fds, fdr, hxs, hxr,
-    zus, zur, zds, zdr, rs, rr, a_s, a_r, b_s, b_r,
+    send_a, recv_a, send_b, recv_b, wide_a, wide_b, send_c, recv_c, recv_d, send_d, small, old,
+    loc, w1s, w1r, h1s, h1r, ups, upr, dns, dnr, hfs, hfr, hxs, hxr,
+    zus, zur, zds, zdr, rs, rr, a_s, a_r, b_s, b_r, c_s, c_r, d_s, d_r,
 ):
     sect, dp, tp = lax.axis_index("sect"), lax.axis_index("dp"), lax.axis_index("tp")
     z_hi, x, core = dp // 8, (dp // 2) % 4, dp % 2
@@ -132,7 +133,7 @@
             h_stage.at[(x + k) % NX], acts.at[tp, tokens(x, core), :], h1s.at[k - 1], h1r.at[k - 1], device(dx=k)
         )
 
-    hup, hdn, hfu, hfd, hx = {}, {}, {}, {}, {}
+    hup, hdn, hfar, hx = {}, {}, {}, {}
 
     def chunk(dy, k):
         return acts.at[(tp + dy + NY) % NY, tokens((x - k + NX) % NX, core), :]
@@ -145,18 +146,22 @@
         ref = chunk(0, k)
         hup[k] = send(ref, ref, ups.at[k], upr.at[k], device(dy=1))
         hdn[k] = send(ref, ref, dns.at[k], dnr.at[k], device(dy=-1))
+        if k in STRAIGHT:
+            hfar[k] = send(ref, ref, hfs.at[k], hfr.at[k], device(dy=2))
         hcore(0, k)
 
     def yforward(k):
         if k % 2 == 0:
             hup[k].wait_recv()
             ref = chunk(-1, k)
-            hfu[k] = send(ref, ref, fus.at[k // 2], fur.at[k // 2], device(dy=1))
+            if k not in STRAIGHT:
+                hfar[k] = send(ref, ref, hfs.at[k], hfr.at[k], device(dy=1))
             hcore(-1, k)
         else:
             hdn[k].wait_recv()
             ref = chunk(1, k)
-            hfd[k] = send(ref, ref, fds.at[k // 2], fdr.at[k // 2], device(dy=-1))
+            if k not in STRAIGHT:
+                hfar[k] = send(ref, ref, hfs.at[k], hfr.at[k], device(dy=-1))
             hcore(1, k)
 
     def yother(k):
@@ -168,7 +173,7 @@
             hcore(-1, k)
 
     def ylast(k):
-        (hfu if k % 2 == 0 else hfd)[k].wait_recv()
+        hfar[k].wait_recv()
         hcore(2, k)
 
     for k in (2, 1, 3, 0):
@@ -202,110 +207,10 @@
         top = jnp.max(score, axis=1, keepdims=True)
         e = jnp.exp2(score - top)
         total = jnp.sum(e, axis=1, keepdims=True)
-        oc[kv, rows, :] = jnp.dot(e.astype(jnp.bfloat16), vals, preferred_element_type=jnp.float32)
-        mc[kv, rows, :] = jnp.broadcast_to(top, (128, HEAD))
-        lc[kv, rows, :] = jnp.broadcast_to(total, (128, HEAD))
-
-    row = lax.broadcasted_iota(jnp.int32, (256, 256), 0)
-    pick[...] = jnp.where(row == slots[...], 1.0, 0.0).astype(jnp.bfloat16)
-
-    for copy in own_q:
-        copy.wait()
-    over_cache(0, 0)
-
-    def wfirst(k):
-        for o in range(2):
-            w1[k, o].wait_recv()
-        zfirst(k)
-
-    def hfirst(k):
-        h1[k].wait_recv()
-        ysend(k)
-
-    over_cache(0, 1)
-    wfirst(1)
-    wfirst(3)
-    zpass(0, 1)
-    wfirst(2)
-    hfirst(1)
-    hfirst(3)
-    yforward(0)
-    hfirst(2)
-    zpass(1, 1)
-    zpass(3, 1)
-    yother(0)
-    zpass(0, 2)
-    zpass(2, 1)
-    yforward(1)
-    yforward(3)
-    yforward(2)
-    zpass(1, 2)
-    zpass(3, 2)
-    for k in (1, 3, 2):
-        yother(k)
-    zpass(0, 3)
-    zpass(2, 2)
-    for k in (0, 1, 3, 2):
-        ylast(k)
-    zpass(0, 4)
-    for k in (1, 3, 2):
-        zpass(k, 3)
-        zpass(k, 4)
-    for copy in hx.values():
-        copy.wait_recv()
-
-    total = None
-    for y in range(NY):
-        term = jnp.dot(
-            acts[y], weights[2 * y : 2 * y + 2].reshape(512, 256), preferred_element_type=jnp.float32
-        )
-        total = term if total is None else total + term
-    part[...] = total.reshape(2, NX, TOK, 256)
-    part_send[...] = total.reshape(2, NX, TOK, 256).astype(jnp.bfloat16)
-    sums = [
-        send(
-            part_send.at[there if o else core, (x + k) % NX], part_recv.at[o, k],
-            rs.at[o, k], rr.at[o, k], device(dx=k, other=o == 1),
-        )
-        for k in (2, 1, 3, 0)
-        for o in range(2)
-        if k or o
-    ]
-    over_cache(1, 0)
-    over_cache(1, 1)
-    over_cache(2, 0)
-    over_cache(2, 1)
-    over_cache(3, 0)
-    over_cache(3, 1)
-    for copy in sums:
-        copy.wait_recv()
-    same, cross = part[core, x], part_recv[1, 0].astype(jnp.float32)
-    for k in range(1, NX):
-        same = same + part_recv[0, k].astype(jnp.float32)
-        cross = cross + part_recv[1, k].astype(jnp.float32)
-    fresh[core] = same.astype(jnp.bfloat16)
-    fresh[there] = cross.astype(jnp.bfloat16)
-
-    r = lax.broadcasted_iota(jnp.int32, (512, TOK), 0)
-    j = lax.broadcasted_iota(jnp.int32, (512, TOK), 1)
-    seen = (r // 128 == j // STEPS) & (j % STEPS <= r % STEPS)
-    step = lax.broadcasted_iota(jnp.int32, (128, HEAD), 0) % STEPS
-    for kv in range(2):
-        keys = fresh[0, :, kv * HEAD : (kv + 1) * HEAD]
-        vals = fresh[1, :, kv * HEAD : (kv + 1) * HEAD]
-        score = lax.dot_general(qrows[kv], keys, (((1,), (1,)), ((), ())), preferred_element_type=jnp.float32)
-        score = jnp.where(seen, score * scale, NEG)
-        old = mc[kv]
-        top = jnp.maximum(old, jnp.broadcast_to(jnp.max(score, axis=1, keepdims=True), (512, HEAD)))
-        e = jnp.exp2(score - top[:, :TOK])
-        shrink = jnp.exp2(old - top)
-        denom = lc[kv] * shrink + jnp.broadcast_to(jnp.sum(e, axis=1, keepdims=True), (512, HEAD))
-        value = oc[kv] * shrink + jnp.dot(e.astype(jnp.bfloat16), vals, preferred_element_type=jnp.float32)
-        value = value / denom
-        for n in range(SEQ):
-            oc[kv, n * 128 : (n + 1) * 128, :] = jnp.where(step < rolls[n], value[n * 128 : (n + 1) * 128], 0.0)
-        for q in range(32):
-            send_a[kv * 32 + q] = oc[kv, pl.ds(q, 16, stride=32), :].astype(jnp.bfloat16)
+        value = jnp.dot(e.astype(jnp.bfloat16), vals, preferred_element_type=jnp.float32)
+        oc[kv, rows, :] = value / total
+        mc[kv * SEQ + n, :, :] = jnp.transpose(jnp.broadcast_to(top, (128, HEAD)))[:8]
+        lc[kv * SEQ + n, :, :] = jnp.transpose(jnp.broadcast_to(total, (128, HEAD)))[:8]
 
     def spread(src, dst, s_sem, r_sem):
         for dx in (2, 1, 3, 0):
@@ -323,25 +228,208 @@
         some = buf.at[pl.ds(0, HOLDERS - 1)]
         pltpu.make_async_copy(some, some, sem).wait()
 
+    row = lax.broadcasted_iota(jnp.int32, (256, 256), 0)
+    pick[...] = jnp.where(row == slots[...], 1.0, 0.0).astype(jnp.bfloat16)
+
+    for copy in own_q:
+        copy.wait()
+    over_cache(0, 0)
+
+    def wfirst(k):
+        for o in range(2):
+            w1[k, o].wait_recv()
+        zfirst(k)
+
+    def hfirst(k):
+        h1[k].wait_recv()
+        ysend(k)
+
+    def tiles(kv):
+        for q in range(32):
+            send_a[kv * 32 + q] = oc[kv, pl.ds(q, 16, stride=32), :].astype(jnp.bfloat16)
+
+    wfirst(1)
+    wfirst(3)
+    zpass(0, 1)
+    wfirst(2)
+    hfirst(1)
+    hfirst(3)
+    yforward(0)
+    hfirst(2)
+    over_cache(1, 0)
+    over_cache(2, 0)
+    zpass(1, 1)
+    zpass(3, 1)
+    yother(0)
+    zpass(0, 2)
+    zpass(2, 1)
+    yforward(1)
+    yforward(3)
+    yforward(2)
+    over_cache(3, 0)
+    tiles(0)
+    over_cache(0, 1)
+    over_cache(1, 1)
+    zpass(1, 2)
+    zpass(3, 2)
+    for k in (1, 3, 2):
+        yother(k)
+    zpass(0, 3)
+    zpass(2, 2)
+    over_cache(2, 1)
+    over_cache(3, 1)
+    tiles(1)
+    for k in (0, 1, 3, 2):
+        ylast(k)
+    zpass(0, 4)
+    for k in (1, 3, 2):
+        zpass(k, 3)
+    for k in (1, 3, 2):
+        zpass(k, 4)
+    for copy in hx.values():
+        copy.wait_recv()
+
     spread(send_a, recv_a, a_s, a_r)
+    total = None
+    for y in range(NY):
+        term = jnp.dot(
+            acts[y], weights[2 * y : 2 * y + 2].reshape(512, 256), preferred_element_type=jnp.float32
+        )
+        total = term if total is None else total + term
+    part[...] = total.reshape(2, NX, TOK, 256)
+    part_send[...] = total.reshape(2, NX, TOK, 256).astype(jnp.bfloat16)
+    sums = [
+        send(
+            part_send.at[there if o else core, (x + k) % NX], part_recv.at[o, k],
+            rs.at[o, k], rr.at[o, k], device(dx=k, other=o == 1),
+        )
+        for k in (2, 1, 3, 0)
+        for o in range(2)
+        if k or o
+    ]
+    for copy in sums:
+        copy.wait_recv()
+    same, cross = part[core, x], part_recv[1, 0].astype(jnp.float32)
+    for k in range(1, NX):
+        same = same + part_recv[0, k].astype(jnp.float32)
+        cross = cross + part_recv[1, k].astype(jnp.float32)
+    fresh[core] = same.astype(jnp.bfloat16)
+    fresh[there] = cross.astype(jnp.bfloat16)
+
+    r = lax.broadcasted_iota(jnp.int32, (STEPS, 128), 1) % STEPS
+    seen = lax.broadcasted_iota(jnp.int32, (STEPS, 128), 0) <= r
+    small[16 * 16 :, :] = jnp.zeros((16, HEAD), jnp.float32)
+    for kv in range(2):
+        for n in range(SEQ):
+            keys = fresh[0, n * STEPS : (n + 1) * STEPS, kv * HEAD : (kv + 1) * HEAD]
+            score = lax.dot_general(
+                keys, qrows[kv, n * 128 : (n + 1) * 128, :], (((1,), (1,)), ((), ())),
+                preferred_element_type=jnp.float32,
+            )
+            score = jnp.where(seen, score * scale, NEG)
+            before = mc[kv * SEQ + n, 0:1, :]
+            top = jnp.maximum(before, jnp.max(score, axis=0, keepdims=True))
+            e = jnp.exp2(score - top)
+            cached = lc[kv * SEQ + n, 0:1, :] * jnp.exp2(before - top)
+            factor = 1.0 / (cached + jnp.sum(e, axis=0, keepdims=True))
+            factor = jnp.where(r[0:1, :] < rolls[n], factor, 0.0)
+            small[pl.ds(kv * TOK + n * STEPS, STEPS), :] = e * factor
+            small[pl.ds(16 * 16 + n * 4 + kv, 1), :] = cached * factor
+        small[pl.ds((2 + kv) * TOK, TOK), :] = fresh[1, :, kv * HEAD : (kv + 1) * HEAD].astype(jnp.float32)
+    for part_ in range(4):
+        for jq in range(4):
+            send_c[part_ * 4 + jq] = small[pl.ds(part_ * TOK + jq, 16, stride=4), :].astype(jnp.bfloat16)
+    send_c[16] = small[pl.ds(16 * 16, 16), :].astype(jnp.bfloat16)
+
+    def middle(t):
+        zp = t // 2 if t < 16 else 0
+        xp = (t % 2) * 2 + zp % 2 if t < 16 else 1
+        c = 0 if t < 16 else 1
+        return zp % 2, (zp // 2) * 8 + xp * 2 + c
+
+    places = [middle(t) for t in range(17)]
+    middles = [a * 32 + b for a, b in places]
+    mine = functools.reduce(jnp.logical_or, [me == m for m in middles])
+    for t in sorted(range(17), key=lambda t: -t):
+        @pl.when(me != middles[t])
+        def _(t=t):
+            pltpu.make_async_remote_copy(
+                src_ref=send_c.at[t], dst_ref=recv_c.at[me], send_sem=c_s, recv_sem=c_r,
+                device_id=(*places[t], tp), device_id_type=MESH,
+            ).start()
+
+        @pl.when(me == middles[t])
+        def _(t=t):
+            recv_c[me] = send_c[t]
+
+    def wait_tiles(buf, sem, count):
+        some = buf.at[pl.ds(0, count)]
+        pltpu.make_async_copy(some, some, sem).wait()
+
+    def reorder(src, dst):
+        wide_a[...] = src[...].reshape(1024, HEAD).astype(jnp.float32)
+        for u in range(4):
+            pieces = wide_a[pl.ds(u, 256, stride=4), :].astype(jnp.bfloat16)
+            wide_b[pl.ds(u, 256, stride=4), :] = jnp.dot(pick[...], pieces, preferred_element_type=jnp.float32)
+        dst[...] = wide_b[...].astype(jnp.bfloat16).reshape(HOLDERS, 16, HEAD)
+
     arrived(recv_a, a_r)
-    wide_a[...] = recv_a[...].reshape(1024, HEAD).astype(jnp.float32)
-    for u in range(4):
-        pieces = wide_a[pl.ds(u, 256, stride=4), :].astype(jnp.bfloat16)
-        wide_b[pl.ds(u, 256, stride=4), :] = jnp.dot(pick[...], pieces, preferred_element_type=jnp.float32)
-    send_b[...] = wide_b[...].astype(jnp.bfloat16).reshape(HOLDERS, 16, HEAD)
+    reorder(recv_a, send_b)
     spread(send_b, recv_b, b_s, b_r)
+
+    @pl.when(mine)
+    def _():
+        wait_tiles(recv_c, c_r, HOLDERS - 1)
+        reorder(recv_c, send_d)
+        tile = jnp.where(core == 1, 16, 2 * z + x // 2)
+        for dx in (2, 1, 3, 0):
+            for dz in (4, 3, 5, 2, 6, 1, 7, 0):
+                for o in (False, True):
+                    if dz or dx or o:
+                        to = device(dx=dx, dz=dz, other=o)
+                        pltpu.make_async_remote_copy(
+                            src_ref=send_d.at[to[0] * 32 + to[1]], dst_ref=recv_d.at[tile], send_sem=d_s, recv_sem=d_r,
+                            device_id=to, device_id_type=MESH,
+                        ).start()
+        recv_d[tile] = send_d[me]
+
     arrived(recv_b, b_r)
     wide_a[...] = recv_b[...].reshape(1024, HEAD).astype(jnp.float32)
     for kv in range(2):
-        for qh in range(2):
-            for u in range(4):
-                col = (kv * GROUP + 2 * u + qh) * HEAD
-                for n in range(SEQ):
-                    base = (kv * 2 + qh) * 256 + n * 4 + u
-                    out[n * STEPS : (n + 1) * STEPS, col : col + HEAD] = wide_a[
-                        pl.ds(base, 16, stride=16), :
-                    ].astype(jnp.bfloat16)
+        for n in range(SEQ):
+            for g in range(GROUP):
+                old[kv, n, g * STEPS : (g + 1) * STEPS, :] = wide_a[
+                    pl.ds((kv * 2 + g % 2) * 256 + n * 4 + g // 2, 16, stride=16), :
+                ].astype(jnp.bfloat16)
+
+    @pl.when(mine)
+    def _():
+        wait_tiles(recv_d, d_r, 16)
+        wait_tiles(send_c, c_s, 16)
+        wait_tiles(send_d, d_s, HOLDERS - 1)
+
+    @pl.when(jnp.logical_not(mine))
+    def _():
+        wait_tiles(recv_d, d_r, 17)
+        wait_tiles(send_c, c_s, 17)
+
+    small[...] = recv_d[...].reshape(17 * 16, HEAD).astype(jnp.float32)
+    owner = (lax.broadcasted_iota(jnp.int32, (TOK, HEAD), 0) // 4) % 4
+    eye = lax.broadcasted_iota(jnp.int32, (128, 128), 0) == lax.broadcasted_iota(jnp.int32, (128, 128), 1)
+    for kv in range(2):
+        new_w = small[pl.ds(kv * TOK, TOK), :]
+        new_v = small[pl.ds((2 + kv) * TOK, TOK), :].astype(jnp.bfloat16)
+        for n in range(SEQ):
+            share = jnp.broadcast_to(small[pl.ds(16 * 16 + n * 4 + kv, 1), :], (128, 128))
+            value = jnp.dot(jnp.where(eye, share, 0.0).astype(jnp.bfloat16), old[kv, n], preferred_element_type=jnp.float32)
+            value += lax.dot_general(
+                jnp.where(owner == n, new_w, 0.0).astype(jnp.bfloat16), new_v, (((0,), (0,)), ((), ())),
+                preferred_element_type=jnp.float32,
+            )
+            value = value.astype(jnp.bfloat16)
+            for g in range(GROUP):
+                col = (kv * GROUP + g) * HEAD
+                out[n * STEPS : (n + 1) * STEPS, col : col + HEAD] = value[g * STEPS : (g + 1) * STEPS]
     for copy in started:
         copy.wait_send()
     arrived(send_a, a_s)
@@ -370,17 +458,18 @@
         vm((2, TOK, 256), bf),
         vm((2, 512, HEAD), bf),
         vm((2, 512, HEAD), f32),
-        vm((2, 512, HEAD), f32),
-        vm((2, 512, HEAD), f32),
+        vm((2 * SEQ, 8, HEAD), f32),
+        vm((2 * SEQ, 8, HEAD), f32),
         vm((256, 256), bf),
     ]
     scratch += [vm((HOLDERS, 16, HEAD), bf)] * 4 + [vm((1024, HEAD), f32)] * 2
+    scratch += [vm((17, 16, HEAD), bf), vm((HOLDERS, 16, HEAD), bf)] * 2 + [vm((17 * 16, HEAD), f32), vm((2, SEQ, 128, HEAD), bf)]
     scratch += [dma((21,))]
     scratch += [dma((4, 2))] * 2 + [dma((3,))] * 2
-    scratch += [dma((4,))] * 4 + [dma((2,))] * 4 + [dma((4, 4))] * 2
+    scratch += [dma((4,))] * 6 + [dma((4, 4))] * 2
     scratch += [dma((4, 4))] * 4
     scratch += [dma((2, 4))] * 2
-    scratch += [dma] * 4
+    scratch += [dma] * 8
     result = pl.pallas_call(
         kernel,
         out_shape=jax.ShapeDtypeStruct((TOK, 2048), bf),

time: 58.7 us -> 55.4 us (0.944)
  Pallas kernels: 56.9 us -> 53.6 us
    pallas_call x1, Pallas kernels: 56.9 us -> 53.6 us  [shards(): pl.pallas_call(kernel, out_shape=jax.ShapeDtypeStruct((TOK, 2048), bf), i...]
where the time goes in v4:
time: 55.4 us; the launch traced here: 55.3 us
  Pallas kernels  53.6 us (97%)
  local copies, waits for them, and re-layouts  1.67 us (3%)
    pallas_call x1, Pallas kernels, shards(): pl.pallas_call(kernel, out_shape=jax.ShapeDtypeStruct((TOK, 2048), bf), i...  53.6 us
    unnamed x1, local copies, waits for them, and re-layouts  1.67 us

profile of v4, /device:TPU:1, one launch (start us, length us, event | category | flops | bytes accessed | tf_op | source)
XLA Modules:
  0.0 55.3 jit_solution(4280463741317003395)
XLA Ops:
  0.0 53.6 %rollout.1 = bf16[64,2048]{1,0:T(8,128)(2,1)} custom-call(s32[4]{0:T(128)} %lens.1, s32[4]{0:T(128)} %rolls.1, s32[1,256]{1,0:T(1,128)} %bitcast.11, bf16[32,1024]{1,0:T(8,128)(2,1)} %w_key.1, bf16[32,1024]{1,0:T(8,128)(2,1)} %w_value.1, bf16[64,2048]{1,0:T(8,128)(2,1)} %bitcast.9, bf16[64,2048]{1,0:T(8,128)(2,1)} %bitcast.10, bf16[2048,256]{1,0:T(8,128)(2,1)} %bitcast.7, ...), custom_call_target="tpu_custom_call" | custom-call | tf_op jit(solution)/shard_map/rollout/pallas_call | solution.py:473
  53.6 1.7 %copy.11 = bf16[4,16,2048]{2,1,0:T(8,128)(2,1)} copy(bf16[4,16,2048]{2,1,0:T(8,128)(2,1)} %bitcast.6) | data formatting | bytes 524288

commit v5 on v4

--- a/solution.py
+++ b/solution.py
@@ -212,8 +212,8 @@
         mc[kv * SEQ + n, :, :] = jnp.transpose(jnp.broadcast_to(top, (128, HEAD)))[:8]
         lc[kv * SEQ + n, :, :] = jnp.transpose(jnp.broadcast_to(total, (128, HEAD)))[:8]
 
-    def spread(src, dst, s_sem, r_sem):
-        for dx in (2, 1, 3, 0):
+    def spread(src, dst, s_sem, r_sem, columns=(2, 1, 3, 0)):
+        for dx in columns:
             for dz in (4, 3, 5, 2, 6, 1, 7, 0):
                 for o in (False, True):
                     if dz or dx or o:
@@ -222,7 +222,8 @@
                             src_ref=src.at[to[0] * 32 + to[1]], dst_ref=dst.at[me], send_sem=s_sem, recv_sem=r_sem,
                             device_id=to, device_id_type=MESH,
                         ).start()
-        dst[me] = src[me]
+        if 0 in columns:
+            dst[me] = src[me]
 
     def arrived(buf, sem):
         some = buf.at[pl.ds(0, HOLDERS - 1)]
@@ -234,6 +235,9 @@
     for copy in own_q:
         copy.wait()
     over_cache(0, 0)
+    over_cache(1, 0)
+    over_cache(2, 0)
+    over_cache(3, 0)
 
     def wfirst(k):
         for o in range(2):
@@ -256,8 +260,6 @@
     hfirst(3)
     yforward(0)
     hfirst(2)
-    over_cache(1, 0)
-    over_cache(2, 0)
     zpass(1, 1)
     zpass(3, 1)
     yother(0)
@@ -266,7 +268,6 @@
     yforward(1)
     yforward(3)
     yforward(2)
-    over_cache(3, 0)
     tiles(0)
     over_cache(0, 1)
     over_cache(1, 1)

time: 55.4 us -> 55.2 us (level)
  no operation moved by 1% of the time
where the time goes in v5:
time: 55.2 us; the launch traced here: 55.1 us
  Pallas kernels  53.4 us (97%)
  local copies, waits for them, and re-layouts  1.67 us (3%)
    pallas_call x1, Pallas kernels, shards(): pl.pallas_call(kernel, out_shape=jax.ShapeDtypeStruct((TOK, 2048), bf), i...  53.4 us
    unnamed x1, local copies, waits for them, and re-layouts  1.67 us

profile of v5, /device:TPU:1, one launch (start us, length us, event | category | flops | bytes accessed | tf_op | source)
XLA Modules:
  0.0 55.1 jit_solution(2941751153541583156)
XLA Ops:
  0.0 53.4 %rollout.1 = bf16[64,2048]{1,0:T(8,128)(2,1)} custom-call(s32[4]{0:T(128)} %lens.1, s32[4]{0:T(128)} %rolls.1, s32[1,256]{1,0:T(1,128)} %bitcast.11, bf16[32,1024]{1,0:T(8,128)(2,1)} %w_key.1, bf16[32,1024]{1,0:T(8,128)(2,1)} %w_value.1, bf16[64,2048]{1,0:T(8,128)(2,1)} %bitcast.9, bf16[64,2048]{1,0:T(8,128)(2,1)} %bitcast.10, bf16[2048,256]{1,0:T(8,128)(2,1)} %bitcast.7, ...), custom_call_target="tpu_custom_call" | custom-call | tf_op jit(solution)/shard_map/rollout/pallas_call | solution.py:474
  53.4 1.7 %copy.11 = bf16[4,16,2048]{2,1,0:T(8,128)(2,1)} copy(bf16[4,16,2048]{2,1,0:T(8,128)(2,1)} %bitcast.6) | data formatting | bytes 524288

commit v6 on v5

--- a/solution.py
+++ b/solution.py
@@ -22,6 +22,7 @@
 ONWARD = [{1: (1,), 2: (1, 2)}] * 4
 GREET = (-1, 1)
 STRAIGHT = ()
+SLANTED = (1, 3)
 
 
 def kernel(
@@ -71,7 +72,7 @@
 
     partners = [device(dx=k, other=o) for k in range(1, NX) for o in (False, True)]
     partners += [device(dy=k, other=o) for k in range(1, NY) for o in (False, True)] + [device(other=True)]
-    partners += [device(dz=k) for k in GREET]
+    partners += [device(dz=k) for k in GREET] + [device(dx=k, dy=d) for k in SLANTED for d in (-1, 1)]
     barrier = pltpu.get_barrier_semaphore()
     for partner in partners:
         pl.semaphore_signal(barrier, inc=1, device_id=partner, device_id_type=MESH)
@@ -126,14 +127,17 @@
         for hop in ONWARD[k].get(dist, ()):
             zsend(k, dist + hop, hop)
 
-    h1 = {}
+    h1, hup, hdn, hfar, hx = {}, {}, {}, {}, {}
 
     def hsend(k):
         h1[k] = send(
             h_stage.at[(x + k) % NX], acts.at[tp, tokens(x, core), :], h1s.at[k - 1], h1r.at[k - 1], device(dx=k)
         )
-
-    hup, hdn, hfar, hx = {}, {}, {}, {}
+        if k in SLANTED:
+            src, dst = h_stage.at[(x + k) % NX], acts.at[tp, tokens(x, core), :]
+            hup[k] = send(src, dst, ups.at[k], upr.at[k], device(dx=k, dy=1))
+            hdn[k] = send(src, dst, dns.at[k], dnr.at[k], device(dx=k, dy=-1))
+
 
     def chunk(dy, k):
         return acts.at[(tp + dy + NY) % NY, tokens((x - k + NX) % NX, core), :]
@@ -144,8 +148,9 @@
 
     def ysend(k):
         ref = chunk(0, k)
-        hup[k] = send(ref, ref, ups.at[k], upr.at[k], device(dy=1))
-        hdn[k] = send(ref, ref, dns.at[k], dnr.at[k], device(dy=-1))
+        if k not in SLANTED:
+            hup[k] = send(ref, ref, ups.at[k], upr.at[k], device(dy=1))
+            hdn[k] = send(ref, ref, dns.at[k], dnr.at[k], device(dy=-1))
         if k in STRAIGHT:
             hfar[k] = send(ref, ref, hfs.at[k], hfr.at[k], device(dy=2))
         hcore(0, k)

time: 55.2 us -> 54.9 us (level)
  no operation moved by 1% of the time
where the time goes in v6:
time: 54.9 us; the launch traced here: 54.8 us
  Pallas kernels  53.1 us (97%)
  local copies, waits for them, and re-layouts  1.67 us (3%)
    pallas_call x1, Pallas kernels, shards(): pl.pallas_call(kernel, out_shape=jax.ShapeDtypeStruct((TOK, 2048), bf), i...  53.1 us
    unnamed x1, local copies, waits for them, and re-layouts  1.67 us

profile of v6, /device:TPU:1, one launch (start us, length us, event | category | flops | bytes accessed | tf_op | source)
XLA Modules:
  0.0 54.8 jit_solution(7520890738428130132)
XLA Ops:
  0.0 53.1 %rollout.1 = bf16[64,2048]{1,0:T(8,128)(2,1)} custom-call(s32[4]{0:T(128)} %lens.1, s32[4]{0:T(128)} %rolls.1, s32[1,256]{1,0:T(1,128)} %bitcast.11, bf16[32,1024]{1,0:T(8,128)(2,1)} %w_key.1, bf16[32,1024]{1,0:T(8,128)(2,1)} %w_value.1, bf16[64,2048]{1,0:T(8,128)(2,1)} %bitcast.9, bf16[64,2048]{1,0:T(8,128)(2,1)} %bitcast.10, bf16[2048,256]{1,0:T(8,128)(2,1)} %bitcast.7, ...), custom_call_target="tpu_custom_call" | custom-call | tf_op jit(solution)/shard_map/rollout/pallas_call | solution.py:479
  53.1 1.7 %copy.11 = bf16[4,16,2048]{2,1,0:T(8,128)(2,1)} copy(bf16[4,16,2048]{2,1,0:T(8,128)(2,1)} %bitcast.6) | data formatting | bytes 524288
